TPU v7x, 32 devices: a whole 2x2x4 slice. The times are simulated.
32 devices in a mesh: grp: 2 (over x), attn: 8 (over z, y), ffn: 2 (over core).
Axes of the slice: x: 2, y: 2, z: 4, core: 2. Of those that a mesh axis runs over, the one named last changes fastest.
Arguments:
- queries: bfloat16 [64, 8192], P(('grp', 'attn', 'ffn')), parts along dimension 0, may hold values from -125 to 125
- key_cache: bfloat16 [64, 320, 1024], P(('grp', 'attn', 'ffn')), parts along dimension 0, may hold values from -6.1 to 6.1
- value_cache: bfloat16 [64, 320, 1024], P(('grp', 'attn', 'ffn')), parts along dimension 0, may hold values from -6 to 6
- lengths: int32 [64], P(('grp', 'attn', 'ffn')), parts along dimension 0, may hold values from 40 to 320, as said below
- slot_order: int32 [64], P('grp'), parts along dimension 0, may hold values from 0 to 31, each once
- kept_rows: int32 [64], P(('grp', 'ffn')), parts along dimension 0, may hold values 0 or 1
- residual: bfloat16 [64, 8192], P('grp', 'attn'), parts along dimension 0, may hold values from -6 to 6
- norm_gain: float32 [8192], P('attn'), may hold values from 0.1 to 1.9
- w_out: bfloat16 [8192, 8192], P(None, 'attn'), may hold values from -0.0625 to 0.0625
- w_gate: bfloat16 [8192, 16384], P(None, ('attn', 'ffn')), may hold values from -0.0625 to 0.0625
- w_up: bfloat16 [8192, 16384], P(None, ('attn', 'ffn')), may hold values from -0.0625 to 0.0625
- w_down: bfloat16 [16384, 8192], P(('attn', 'ffn')), may hold values from -0.0625 to 0.0625
Outputs:
- mixed: bfloat16 [64, 8192], P(('grp', 'ffn'), 'attn'), parts along dimension 0
There are 2 independent parts, one for each index of `grp`. A program takes and returns all parts, laid end to end along the dimension named above; an argument that names none is the same for every part. Nothing has to cross between parts.
Inputs may be any that keep to these rules, and one draw needn't show every extreme that they name: `lengths`: every slot has at least 40 live entries and some slot has exactly 320.
All inputs are finite; a program needn't handle non-finite values. No bound on the sum of `kept_rows` on one device may be relied on, other than what follows from the above.
Results may differ from a plain program's by a relative error of at most 0.006.
Values may be sent and summed in bfloat16 or wider, within the bound.
A program may use at most 192 MiB of HBM per device.

v0:
```python
import jax
import jax.numpy as jnp
from jax import lax
from jax.sharding import PartitionSpec as P

D = 8192
QH = 64
KVH = 8
HD = 128


NEG_BIG = -1e30
EPSILON = 1e-05


def local_attention(queries, key_cache, value_cache, lengths):
    row_count = queries.shape[0]
    slot_count = key_cache.shape[1]
    grouped = queries.reshape(row_count, KVH, QH // KVH, HD)
    key_rows = key_cache.reshape(row_count, slot_count, KVH, HD)
    value_rows = value_cache.reshape(row_count, slot_count, KVH, HD)
    scores = jnp.einsum(
        "rkgd,rpkd->rkgp", grouped, key_rows, preferred_element_type=jnp.float32
    ) * HD ** (-0.5)
    in_range = (jnp.arange(slot_count, dtype=jnp.int32)[None, :] < lengths[:, None])[
        :, None, None, :
    ]
    scores = jnp.where(in_range, scores, NEG_BIG)
    largest = jnp.max(scores, axis=3)
    exponent = jnp.where(in_range, jnp.exp(scores - largest[..., None]), 0.0)
    totals = jnp.sum(exponent, axis=3)
    weighted = jnp.einsum(
        "rkgp,rpkd->rkgd",
        exponent.astype(jnp.bfloat16),
        value_rows,
        preferred_element_type=jnp.float32,
    )
    return (weighted / totals[..., None]).reshape(row_count, -1).astype(jnp.bfloat16)


def per_device(
    queries,
    key_cache,
    value_cache,
    lengths,
    slot_order,
    kept_rows,
    residual,
    norm_gain,
    w_out,
    w_gate,
    w_up,
    w_down,
):
    context = local_attention(queries, key_cache, value_cache, lengths)
    attended = jnp.dot(
        lax.all_gather(context, ("attn", "ffn"), axis=0, tiled=True),
        w_out,
        preferred_element_type=jnp.float32,
    )
    hidden = residual.astype(jnp.float32) + jnp.take(attended, slot_order, axis=0)
    squares = lax.psum(jnp.sum(hidden * hidden, axis=1), "attn")
    normed = (hidden * lax.rsqrt(squares / D + EPSILON)[:, None] * norm_gain).astype(jnp.bfloat16)
    all_rows = normed.shape[0]
    segment = lax.all_gather(normed, "attn", axis=1, tiled=True)
    gate_sum = jnp.dot(segment, w_gate, preferred_element_type=jnp.float32)
    up_sum = jnp.dot(segment, w_up, preferred_element_type=jnp.float32)
    activated = (jax.nn.silu(gate_sum) * up_sum).astype(jnp.bfloat16)
    partial_out = jnp.dot(activated, w_down, preferred_element_type=jnp.float32)
    share_rows = all_rows // lax.axis_size("ffn")
    summed = lax.psum_scatter(partial_out, "attn", scatter_dimension=1, tiled=True)
    summed = lax.psum_scatter(summed, "ffn", scatter_dimension=0, tiled=True)
    own_hidden = lax.dynamic_slice_in_dim(hidden, lax.axis_index("ffn") * share_rows, share_rows, 0)
    return (own_hidden + kept_rows.astype(jnp.float32)[:, None] * summed).astype(jnp.bfloat16)


def solution(mesh):
    return jax.shard_map(
        per_device,
        mesh=mesh,
        in_specs=(
            P(("grp", "attn", "ffn"), None),
            P(("grp", "attn", "ffn"), None, None),
            P(("grp", "attn", "ffn"), None, None),
            P(("grp", "attn", "ffn")),
            P("grp"),
            P(("grp", "ffn")),
            P("grp", "attn"),
            P("attn"),
            P(None, "attn"),
            P(None, ("attn", "ffn")),
            P(None, ("attn", "ffn")),
            P(("attn", "ffn"), None),
        ),
        out_specs=P(("grp", "ffn"), "attn"),
        check_vma=False,
    )
```

profile of v0, /device:TPU:0, one launch (start us, length us, event | category | flops | bytes accessed | tf_op | source)
XLA Modules:
  0.0 198.3 jit_solution(4382665393106948298)
XLA Ops:
  6.5 0.0 copy-start
  6.5 0.0 copy-start.2
  6.5 0.0 copy-start.3
  6.5 0.0 reduce-scatter.3.cloned.1.call-start
  6.5 0.8 compare_select_fusion
  7.3 0.7 compare_and_fusion
  8.0 0.7 iota_compare_fusion
  8.7 0.0 copy-done
  8.7 1.3 fusion.11
  10.0 0.2 fusion.34
  10.2 1.7 fusion.20
  11.9 24.6 %all-gather = bf16[16,2,8192]{2,1,0:T(2,128)(2,1)S(1)} all-gather(bf16[1,2,8192]{2,1,0:T(2,128)(2,1)S(1)} %reshape.50), channel_id=1, replica_groups=mesh['grp'=2,'attn'=8,'ffn'=2] {'attn','ffn'}, dimensions={0}, use_global_device_ids=true | all-gather | bytes 557056 | tf_op jit(solution)/shard_map/all_gather | solution.py:57
  36.5 0.2 reshape.51
  36.7 8.7 %fusion.35 = f32[32,1024]{1,0:T(8,128)S(1)} fusion(bf16[32,8192]{1,0:T(8,128)(2,1)S(1)} %reshape.51, bf16[8192,1024]{1,0:T(8,128)(2,1)} %param.20), kind=kOutput, calls=%fused_computation.38 | convolution fusion | flops 536870912 | bytes 17432576 | tf_op jit(solution)/shard_map/dot_general | solution.py:56
  45.5 0.6 gather_fusion
  46.1 0.0 copy-done.2
  46.1 0.2 multiply_reduce_fusion
  46.3 17.1 %psum.7 = f32[32]{0:T(128)S(1)} all-reduce(f32[32]{0:T(128)S(1)} %get-tuple-element.5), channel_id=1, replica_groups=mesh['grp'=2,'attn'=8,'ffn'=2] {'attn'}, use_global_device_ids=true, to_apply=%region_3.4 | all-reduce | flops 32 | bytes 256 | tf_op jit(solution)/shard_map/psum | solution.py:62
  63.4 0.0 copy-done.3
  63.4 0.1 multiply_convert_fusion
  63.5 31.5 %all_gather.7 = bf16[32,8192]{1,0:T(8,128)(2,1)S(1)} all-gather(bf16[32,1024]{1,0:T(8,128)(2,1)S(1)} %multiply_convert_fusion), channel_id=1, replica_groups=mesh['grp'=2,'attn'=8,'ffn'=2] {'attn'}, dimensions={1}, use_global_device_ids=true | all-gather | bytes 589824 | tf_op jit(solution)/shard_map/all_gather | solution.py:65
  95.0 0.0 copy-start.1
  95.0 8.8 %fusion.36 = f32[32,1024]{1,0:T(8,128)S(1)} fusion(bf16[32,8192]{1,0:T(8,128)(2,1)S(1)} %all_gather.7, bf16[8192,1024]{1,0:T(8,128)(2,1)} %param.21), kind=kOutput, calls=%fused_computation.39 | convolution fusion | flops 536870912 | bytes 17432576 | tf_op jit(solution)/shard_map/dot_general | solution.py:66
  103.9 14.6 %fusion.23 = f32[32,8192]{1,0:T(8,128)} fusion(bf16[1024,8192]{1,0:T(8,128)(2,1)} %param.23, bf16[32,8192]{1,0:T(8,128)(2,1)S(1)} %all_gather.7, bf16[8192,1024]{1,0:T(8,128)(2,1)} %param.22, f32[32,1024]{1,0:T(8,128)S(1)} %fusion.36), kind=kOutput, calls=%fused_computation.17 | convolution fusion | flops 1073938432 | bytes 35258368 | tf_op jit(solution)/shard_map/dot_general | solution.py:69
  118.5 0.0 reduce-scatter.3.cloned.1.call-update
  118.5 0.0 reduce-scatter.5.cloned.1.call-start
  118.6 62.5 %reduce-scatter.3.cloned.1.call-done = f32[32,1024]{1,0:T(8,128)} async-done(((f32[32,8192]{1,0:T(8,128)}), f32[32,1024]{1,0:T(8,128)}) %reduce-scatter.3.cloned.1.call-update) | async-done | bytes 131088 | tf_op jit(solution)/shard_map/reduce_scatter | solution.py:71
  181.0 0.0 reduce-scatter.5.cloned.1.call-update
  181.1 0.0 copy-done.4
  181.1 8.8 %reduce-scatter.5.cloned.1.call-done = f32[16,1024]{1,0:T(8,128)} async-done(((f32[32,1024]{1,0:T(8,128)}), f32[16,1024]{1,0:T(8,128)}) %reduce-scatter.5.cloned.1.call-update) | async-done | bytes 65552 | tf_op jit(solution)/shard_map/reduce_scatter | solution.py:72
  189.9 1.5 add_convert_fusion
  191.4 0.0 copy-done.1
  (5 shorter events, 0.0 us)
Async XLA Ops:
  6.5 2.2 %copy-start = (bf16[2,320,1024]{2,1,0:T(8,128)(2,1)S(1)}, bf16[2,320,1024]{2,1,0:T(8,128)(2,1)}, u32[]{:S(2)}) copy-start(bf16[2,320,1024]{2,1,0:T(8,128)(2,1)} %param.13) | copy-start | bytes 3932164
  6.5 39.6 %copy-start.2 = (bf16[32,1024]{1,0:T(8,128)(2,1)S(1)}, bf16[32,1024]{1,0:T(8,128)(2,1)}, u32[]{:S(2)}) copy-start(bf16[32,1024]{1,0:T(8,128)(2,1)} %param.18) | copy-start | bytes 196612
  6.5 56.9 %copy-start.3 = (f32[1024]{0:T(1024)S(1)}, f32[1024]{0:T(1024)}, u32[]{:S(2)}) copy-start(f32[1024]{0:T(1024)} %param.19) | copy-start | bytes 12292
  6.5 174.5 %reduce-scatter.3.cloned.1.call-start = ((), (), s32[]{:S(2)}) async-start(), calls=%async_computation.2 | async-start | bytes 1179648 | tf_op jit(solution)/shard_map/reduce_scatter | solution.py:71
  95.0 96.4 %copy-start.1 = (bf16[2,320,1024]{2,1,0:T(8,128)(2,1)S(1)}, bf16[2,320,1024]{2,1,0:T(8,128)(2,1)}, u32[]{:S(2)}) copy-start(bf16[2,320,1024]{2,1,0:T(8,128)(2,1)} %param.13) | copy-start | bytes 3932164
  103.9 77.2 %copy-start.4 = (s32[16]{0:T(128)S(1)}, s32[16]{0:T(128)}, u32[]{:S(2)}) copy-start(s32[16]{0:T(128)} %param.17) | copy-start | bytes 196
  118.5 71.4 %reduce-scatter.5.cloned.1.call-start = ((), (), s32[]{:S(2)}) async-start(), calls=%async_computation.3 | async-start | bytes 196608 | tf_op jit(solution)/shard_map/reduce_scatter | solution.py:72
Sparse Core Ops, SparseCore 0:
  118.6 62.3 reduce-scatter.2
  183.3 6.5 reduce-scatter.4
where the time goes:
time: 199 us; the launch traced here: 198 us
  blocking collectives  73.2 us (37%)
  waiting for transfers between devices  71.3 us (36%)
  matrix products  35.2 us (18%)
  between operations  13.5 us (7%)
  other arithmetic  4.18 us (2%)
    reduce_scatter x1, waiting for transfers between devices, per_device(): lax.psum_scatter(partial_out, 'attn', scatter_dimension=1, tiled=True)  62.5 us
    all_gather x1, blocking collectives, per_device(): segment = lax.all_gather(normed, 'attn', axis=1, tiled=True)  31.5 us
    all_gather x1, blocking collectives, per_device(): lax.all_gather(context, ('attn', 'ffn'), axis=0, tiled=True)  24.6 us
    psum x1, blocking collectives, per_device(): squares = lax.psum(jnp.sum(hidden * hidden, axis=1), 'attn')  17.1 us
    dot_general x1, matrix products, per_device(): partial_out = jnp.dot(activated, w_down, preferred_element_type=jnp.float32)  14.6 us
    dot_general x1, matrix products, per_device(): gate_sum = jnp.dot(segment, w_gate, preferred_element_type=jnp.float32)  8.85 us
    reduce_scatter x1, waiting for transfers between devices, per_device(): summed = lax.psum_scatter(summed, 'ffn', scatter_dimension=0, tiled=True)  8.81 us
    dot_general x1, matrix products, per_device(): jnp.dot(lax.all_gather(context, ('attn', 'ffn'), axis=0, tiled=True), w_o...  8.75 us
  transfers between devices with their start and end apart: 2, of which 2 were waited for; matrix products, arithmetic and copies ran while one was open for 0% of the time, Pallas kernels for 0%

commit v1 on v0

--- a/solution.py
+++ b/solution.py
@@ -1,6 +1,8 @@
 import jax
 import jax.numpy as jnp
 from jax import lax
+from jax.experimental import pallas as pl
+from jax.experimental.pallas import tpu as pltpu
 from jax.sharding import PartitionSpec as P
 
 D = 8192
@@ -74,9 +76,364 @@
     return (own_hidden + kept_rows.astype(jnp.float32)[:, None] * summed).astype(jnp.bfloat16)
 
 
+MESH = pl.DeviceIdType.MESH
+F32 = jnp.float32
+BF16 = jnp.bfloat16
+ZN = 4
+NDEV = 16
+ROWS = 32
+HALF = 16
+SPLIT = 512
+
+
+def iota(shape, dim):
+    return lax.broadcasted_iota(jnp.int32, shape, dim)
+
+
+def fused_kernel(
+    queries, keys, values, lengths, slot_order, kept_rows, residual, gain, w_out, w_gate, w_up, w_down,
+    out,
+    kbuf, vbuf, qbd, ctx, sel, pcx, pool, gbuf, ubuf, xbuf, acc_g, acc_u, hidden, hid_own, act,
+    part, s1_send, s1_recv, s2_send, s2_recv, s3_send, s3_recv,
+    kv_sem, pool_sem, down_sem, gate_sem, up_sem,
+    ctx_send, ctx_recv, x_send, x_recv, hid_sem, s1_ssem, s1_rsem, s2_ssem, s2_rsem, s3_ssem, s3_rsem,
+):
+    attn = lax.axis_index("attn")
+    c = lax.axis_index("ffn")
+    z, y = attn // 2, attn % 2
+    oz = lambda j: (z + j) % ZN
+    block = lambda zz, yy, cc: (zz * 2 + yy) * 2 + cc
+    core_id = {"attn": attn, "ffn": 1 - c}
+    y_id = {"attn": z * 2 + 1 - y, "ffn": c}
+    z_id = lambda j: {"attn": oz(j) * 2 + y, "ffn": c}
+
+    def remote(src, dst, ssem, rsem, dev):
+        return pltpu.make_async_remote_copy(
+            src_ref=src, dst_ref=dst, send_sem=ssem, recv_sem=rsem, device_id=dev, device_id_type=MESH
+        )
+
+    barrier = pltpu.get_barrier_semaphore()
+    for dev in (core_id, y_id, z_id(1), z_id(2), z_id(3)):
+        pl.semaphore_signal(barrier, inc=1, device_id=dev, device_id_type=MESH)
+
+    def kv_load(r):
+        return (
+            pltpu.make_async_copy(keys.at[r], kbuf.at[r], kv_sem.at[0, r]),
+            pltpu.make_async_copy(values.at[r], vbuf.at[r], kv_sem.at[1, r]),
+        )
+
+    def out_load(k):
+        return pltpu.make_async_copy(
+            w_out.at[pl.ds(k * 1024, 1024), pl.ds(pl.multiple_of(c * SPLIT, SPLIT), SPLIT)],
+            pool.at[k],
+            pool_sem.at[k],
+        )
+
+    def step_block(s):
+        kind, j = s // ZN, s % ZN
+        yy = (y + kind % 2) % 2
+        cc = (c + kind // 2) % 2
+        return block(oz(j), yy, cc)
+
+    def gate_load(s):
+        b = step_block(s)
+        rows = pl.ds(pl.multiple_of(b * SPLIT, SPLIT), SPLIT)
+        return (
+            pltpu.make_async_copy(w_gate.at[rows], gbuf.at[s], gate_sem.at[s]),
+            pltpu.make_async_copy(w_up.at[rows], ubuf.at[s], up_sem.at[s]),
+        )
+
+    def down_load(i):
+        q = i // 2
+        t = oz(1 + q % ZN) * 2 + (y + 1 + q // ZN) % 2
+        col = pl.multiple_of(t * 1024 + (i % 2) * SPLIT, SPLIT)
+        slot = (i + 8) % 16
+        return pltpu.make_async_copy(w_down.at[:, pl.ds(col, SPLIT)], pool.at[slot], down_sem.at[i])
+
+    def start_loop(n, first, load):
+        @pl.loop(first, n)
+        def _(i):
+            copies = load(i)
+            for copy in copies if isinstance(copies, tuple) else (copies,):
+                copy.start()
+
+    for r in range(2):
+        for copy in kv_load(r):
+            copy.start()
+    start_loop(8, 0, out_load)
+
+    order = jnp.zeros((ROWS, 256), jnp.int32)
+    sub = iota((ROWS, 256), 0)
+    lane = iota((ROWS, 256), 1)
+    for i in range(ROWS):
+        order = jnp.where(sub == i, slot_order[i], order)
+    for k in range(KVH):
+        sel[k] = jnp.where(lane == order * 8 + k, 1.0, 0.0).astype(BF16)
+
+    row8 = iota((8, HD), 0)
+    for r in range(2):
+        q_row = queries[...].astype(F32)[r : r + 1]
+        for g in range(8):
+            tiles = [
+                jnp.where(
+                    row8 == k,
+                    jnp.broadcast_to(q_row[:, (k * 8 + g) * HD : (k * 8 + g + 1) * HD], (8, HD)),
+                    0.0,
+                )
+                for k in range(KVH)
+            ]
+            qbd[r, pl.ds(g * 8, 8), :] = jnp.concatenate(tiles, axis=1)
+
+    me = block(z, y, c)
+    rows_out = []
+    for r in range(2):
+        for copy in kv_load(r):
+            copy.wait()
+        if r == 1:
+            start_loop(NDEV, 0, gate_load)
+        scores = lax.dot_general(
+            qbd[r].astype(BF16), kbuf[r], (((1,), (1,)), ((), ())), preferred_element_type=F32
+        ) * HD ** (-0.5)
+        live = iota(scores.shape, 1) < lengths[r]
+        scores = jnp.where(live, scores, NEG_BIG)
+        largest = jnp.max(scores, axis=1, keepdims=True)
+        exponent = jnp.where(live, jnp.exp(scores - largest), 0.0)
+        totals = jnp.sum(exponent, axis=1, keepdims=True)
+        weighted = jnp.dot(exponent.astype(BF16), vbuf[r], preferred_element_type=F32) / totals
+        pieces = []
+        for g in range(8):
+            tile = jnp.zeros((8, HD), F32)
+            for k in range(KVH):
+                tile = jnp.where(row8 == k, weighted[g * 8 : (g + 1) * 8, k * HD : (k + 1) * HD], tile)
+            pieces.append(tile)
+        rows_out.append(jnp.concatenate(pieces, axis=1))
+    ctx[me] = jnp.concatenate(rows_out, axis=0).astype(BF16)
+    start_loop(8, 0, down_load)
+    pl.semaphore_wait(barrier, 5)
+
+    def gather_copies(buf, send, recv):
+        def copy(b, k, dev):
+            return remote(buf.at[b], buf.at[b], send.at[k], recv.at[b], dev)
+
+        to_z = lambda j: copy(me, j - 1, z_id(j))
+        to_y = lambda j: copy(block(oz(j), y, c), 3 + j, y_id)
+        to_core = lambda kind, j: copy(block(oz(j), (y + kind) % 2, c), 7 + kind * ZN + j, core_id)
+
+        def arrived(b):
+            copy(b, 0, core_id).wait_recv()
+
+        return to_z, to_y, to_core, arrived
+
+    def gather(buf, send, recv, use):
+        to_z, to_y, to_core, arrived = gather_copies(buf, send, recv)
+        for j in (1, 3, 2):
+            to_z(j).start()
+        to_y(0).start()
+        to_core(0, 0).start()
+        use(0)
+
+        @pl.loop(1, ZN)
+        def _(j):
+            arrived(block(oz(j), y, c))
+            to_y(j).start()
+            to_core(0, j).start()
+            use(j)
+
+        @pl.loop(0, ZN)
+        def _(j):
+            arrived(block(oz(j), 1 - y, c))
+            to_core(1, j).start()
+            use(ZN + j)
+
+        @pl.loop(2 * ZN, 4 * ZN)
+        def _(s):
+            arrived(step_block(s))
+            use(s)
+
+    def gather_end(buf, send, recv):
+        to_z, to_y, to_core, _ = gather_copies(buf, send, recv)
+        for j in range(1, ZN):
+            to_z(j).wait_send()
+        for j in range(ZN):
+            to_y(j).wait_send()
+            to_core(0, j).wait_send()
+            to_core(1, j).wait_send()
+
+    gather(ctx, ctx_send, ctx_recv, lambda s: None)
+
+    picked = jnp.dot(
+        sel[...].reshape(256, 256), ctx[...].reshape(256, 1024), preferred_element_type=F32
+    )
+    pcx[...] = picked.astype(BF16).reshape(KVH, ROWS, 1024)
+
+    attended = jnp.zeros((ROWS, SPLIT), F32)
+
+    def out_step(k, total):
+        out_load(k).wait()
+        return total + jnp.dot(pcx[k], pool[k], preferred_element_type=F32)
+
+    attended = lax.fori_loop(0, KVH, out_step, attended)
+    mine = pl.ds(pl.multiple_of(c * SPLIT, SPLIT), SPLIT)
+    hid = residual[:, mine].astype(F32) + attended
+    square = jnp.sum(hid * hid, axis=1, keepdims=True)
+    high = square.astype(BF16).astype(F32)
+    mid = (square - high).astype(BF16).astype(F32)
+    low = square - high - mid
+    lane128 = iota((ROWS, 128), 1)
+    tail = jnp.where(lane128 == 0, high, jnp.where(lane128 == 1, mid, jnp.where(lane128 == 2, low, 0.0)))
+    xbuf[me, :, :SPLIT] = (hid * gain[:, mine]).astype(BF16)
+    xbuf[me, :, SPLIT:] = tail.astype(BF16)
+    hidden[...] = hid.reshape(2, HALF, SPLIT)
+    acc_g[...] = jnp.zeros_like(acc_g)
+    acc_u[...] = jnp.zeros_like(acc_u)
+
+    @pl.loop(8, 16)
+    def _(i):
+        down_load(i).start()
+
+    def gate_step(s):
+        for copy in gate_load(s):
+            copy.wait()
+        x = xbuf[step_block(s), :, :SPLIT]
+        acc_g[...] += jnp.dot(x, gbuf[s], preferred_element_type=F32)
+        acc_u[...] += jnp.dot(x, ubuf[s], preferred_element_type=F32)
+
+    gather(xbuf, x_send, x_recv, gate_step)
+
+    hid_copy = remote(hidden.at[1 - c], hid_own.at[c], hid_sem.at[0], hid_sem.at[1], core_id)
+    hid_copy.start()
+    hid_own[c] = hidden[c]
+
+    square = jnp.sum(jnp.sum(xbuf[:, :, SPLIT:].astype(F32), axis=0), axis=1, keepdims=True)
+    scale = lax.rsqrt(square / D + EPSILON)
+    gate = acc_g[...] * scale
+    up = acc_u[...] * scale
+    act[...] = (gate / (1.0 + jnp.exp(-gate)) * up).astype(BF16)
+
+    def s1_copy(q):
+        return remote(s1_send.at[q], s1_recv.at[q], s1_ssem.at[q], s1_rsem.at[q], core_id)
+
+    def s2_copy(u):
+        return remote(s2_send.at[u], s2_recv.at[u], s2_ssem.at[u], s2_rsem.at[u], y_id)
+
+    def s3_copy(u):
+        return remote(s3_send.at[u], s3_recv.at[u], s3_ssem.at[u], s3_rsem.at[u], z_id(1 + u))
+
+    def down_step(q):
+        for half in range(2):
+            down_load(2 * q + half).wait()
+            piece = jnp.dot(act[...], pool[(2 * q + half + 8) % 16], preferred_element_type=F32)
+            part[q, :, :, half * SPLIT : (half + 1) * SPLIT] = piece.reshape(2, HALF, SPLIT)
+        s1_send[q] = part[q, 1 - c].astype(BF16)
+        s1_copy(q).start()
+
+    def chip_sum(q):
+        s1_copy(q).wait_recv()
+        return part[q, c] + s1_recv[q].astype(F32)
+
+    def pass_y(u):
+        s2_send[u] = chip_sum(u).astype(BF16)
+        s2_copy(u).start()
+
+    def pair_sum(u):
+        total = chip_sum(ZN + u)
+        s2_copy(u).wait_recv()
+        return total + s2_recv[u].astype(F32)
+
+    down_step(0)
+
+    @pl.loop(1, ZN)
+    def _(q):
+        down_step(q)
+        pass_y(q - 1)
+
+    down_step(ZN)
+    pass_y(ZN - 1)
+
+    @pl.loop(0, ZN - 1)
+    def _(u):
+        down_step(ZN + 1 + u)
+        s3_send[u] = pair_sum(u).astype(BF16)
+        s3_copy(u).start()
+
+    total = pair_sum(ZN - 1)
+    for u in range(ZN - 1):
+        s3_copy(u).wait_recv()
+        total = total + s3_recv[u].astype(F32)
+    kept = jnp.zeros((HALF, 128), jnp.int32)
+    sub16 = iota((HALF, 128), 0)
+    for i in range(HALF):
+        kept = jnp.where(sub16 == i, kept_rows[i], kept)
+    kept = kept.astype(F32)[:, :1]
+    hid_copy.wait()
+    for half in range(2):
+        cols = slice(half * SPLIT, (half + 1) * SPLIT)
+        out[:, cols] = (hid_own[half] + kept * total[:, cols]).astype(BF16)
+
+    gather_end(ctx, ctx_send, ctx_recv)
+    gather_end(xbuf, x_send, x_recv)
+    for q in range(8):
+        s1_copy(q).wait_send()
+    for u in range(ZN):
+        s2_copy(u).wait_send()
+    for u in range(ZN - 1):
+        s3_copy(u).wait_send()
+
+
+def fused_device(
+    queries, key_cache, value_cache, lengths, slot_order, kept_rows, residual, norm_gain, w_out, w_gate, w_up, w_down
+):
+    vmem = pl.BlockSpec(memory_space=pltpu.VMEM)
+    smem = pl.BlockSpec(memory_space=pltpu.SMEM)
+    hbm = pl.BlockSpec(memory_space=pl.ANY)
+    slots = key_cache.shape[1]
+    dma = pltpu.SemaphoreType.DMA
+    return pl.pallas_call(
+        fused_kernel,
+        out_shape=jax.ShapeDtypeStruct((HALF, 1024), BF16),
+        in_specs=[vmem, hbm, hbm, smem, smem, smem, vmem, vmem, hbm, hbm, hbm, hbm],
+        out_specs=vmem,
+        scratch_shapes=[
+            pltpu.VMEM((2, slots, 1024), BF16),
+            pltpu.VMEM((2, slots, 1024), BF16),
+            pltpu.VMEM((2, 64, 1024), F32),
+            pltpu.VMEM((NDEV, 16, 1024), BF16),
+            pltpu.VMEM((KVH, ROWS, 256), BF16),
+            pltpu.VMEM((KVH, ROWS, 1024), BF16),
+            pltpu.VMEM((16, 1024, SPLIT), BF16),
+            pltpu.VMEM((NDEV, SPLIT, 1024), BF16),
+            pltpu.VMEM((NDEV, SPLIT, 1024), BF16),
+            pltpu.VMEM((NDEV, ROWS, SPLIT + 128), BF16),
+            pltpu.VMEM((ROWS, 1024), F32),
+            pltpu.VMEM((ROWS, 1024), F32),
+            pltpu.VMEM((2, HALF, SPLIT), F32),
+            pltpu.VMEM((2, HALF, SPLIT), F32),
+            pltpu.VMEM((ROWS, 1024), BF16),
+            pltpu.VMEM((8, 2, HALF, 1024), F32),
+            pltpu.VMEM((8, HALF, 1024), BF16),
+            pltpu.VMEM((8, HALF, 1024), BF16),
+            pltpu.VMEM((4, HALF, 1024), BF16),
+            pltpu.VMEM((4, HALF, 1024), BF16),
+            pltpu.VMEM((3, HALF, 1024), BF16),
+            pltpu.VMEM((3, HALF, 1024), BF16),
+            dma((2, 2)), dma((8,)), dma((16,)), dma((16,)), dma((16,)),
+            dma((15,)), dma((NDEV,)), dma((15,)), dma((NDEV,)), dma((2,)),
+            dma((8,)), dma((8,)), dma((4,)), dma((4,)), dma((3,)), dma((3,)),
+        ],
+        compiler_params=pltpu.CompilerParams(
+            collective_id=0, has_side_effects=True, vmem_limit_bytes=60 * 1024 * 1024
+        ),
+        cost_estimate=pl.CostEstimate(flops=2 * 32 * 29 * 1024 * 1024, bytes_accessed=60 * 1024 * 1024, transcendentals=0),
+        name="decode_step",
+    )(
+        queries, key_cache, value_cache, lengths, slot_order, kept_rows, residual,
+        norm_gain.reshape(1, -1), w_out, w_gate, w_up, w_down,
+    )
+
+
 def solution(mesh):
     return jax.shard_map(
-        per_device,
+        fused_device if mesh.shape["attn"] == 8 and mesh.shape["ffn"] == 2 else per_device,
         mesh=mesh,
         in_specs=(
             P(("grp", "attn", "ffn"), None),

time: 199 us -> 45.9 us (0.23)
  blocking collectives: 73.2 us -> 0 us
  waiting for transfers between devices: 71.3 us -> 0 us
  Pallas kernels: 0 us -> 44.3 us
  matrix products: 35.2 us -> 0 us
  between operations: 13.5 us -> 0.01 us
  other arithmetic: 4.18 us -> 0 us
    reduce_scatter x2 -> x0, waiting for transfers between devices: 71.3 us -> none  [the longest x1 62.5 us: per_device(): lax.psum_scatter(partial_out, 'attn', scatter_dimension=1, tiled=True)]
    all_gather x2 -> x0, blocking collectives: 56.1 us -> none  [the longest x1 31.5 us: per_device(): segment = lax.all_gather(normed, 'attn', axis=1, tiled=True)]
    pallas_call x0 -> x1, Pallas kernels: none -> 44.3 us  [fused_device(): pl.pallas_call(fused_kernel, out_shape=jax.ShapeDtypeStruct((HALF, 1024),...]
    dot_general x5 -> x0, matrix products: 35.2 us -> none  [the longest x1 14.6 us: per_device(): partial_out = jnp.dot(activated, w_down, preferred_element_type=jnp.float32)]
    psum x1 -> x0, blocking collectives: 17.1 us -> none  [per_device(): squares = lax.psum(jnp.sum(hidden * hidden, axis=1), 'attn')]
  transfers between devices with their start and end apart: 2 -> 0, of which waited for: 2 -> 0; matrix products, arithmetic and copies ran while one was open for 0% -> 0% of each run, Pallas kernels for 0% -> 0%
where the time goes in v1:
time: 45.9 us; the launch traced here: 45.7 us
  Pallas kernels  44.3 us (97%)
  local copies, waits for them, and re-layouts  1.38 us (3%)
    pallas_call x1, Pallas kernels, fused_device(): pl.pallas_call(fused_kernel, out_shape=jax.ShapeDtypeStruct((HALF, 1024),...  44.3 us
    unnamed x1, local copies, waits for them, and re-layouts  1.38 us

profile of v1, /device:TPU:0, one launch (start us, length us, event | category | flops | bytes accessed | tf_op | source)
XLA Modules:
  0.0 45.7 jit_solution(15363574855403798506)
XLA Ops:
  0.0 44.3 %decode_step.1 = bf16[16,1024]{1,0:T(8,128)(2,1)} custom-call(bf16[2,8192]{1,0:T(2,128)(2,1)} %queries.1, bf16[2,320,1024]{2,1,0:T(8,128)(2,1)} %keys.1, bf16[2,320,1024]{2,1,0:T(8,128)(2,1)} %values.1, s32[2]{0:T(128)} %lengths.1, s32[32]{0:T(128)} %slot_order.1, s32[16]{0:T(128)} %kept_rows.1, bf16[32,1024]{1,0:T(8,128)(2,1)} %residual.1, ...), custom_call_target="tpu_custom_call" | custom-call | flops 1946157056 | bytes 62914560 | tf_op jit(solution)/shard_map/decode_step/pallas_call | solution.py:391
  44.3 1.4 %copy.14 = bf16[16,1024]{1,0:T(8,128)(2,1)} copy(bf16[16,1024]{1,0:T(8,128)(2,1)} %decode_step.1) | data formatting | bytes 65536

commit v2 on v1

--- a/solution.py
+++ b/solution.py
@@ -155,7 +155,7 @@
         def _(i):
             copies = load(i)
             for copy in copies if isinstance(copies, tuple) else (copies,):
-                copy.start()
+                copy.start(priority=1)
 
     for r in range(2):
         for copy in kv_load(r):
@@ -289,7 +289,7 @@
 
     @pl.loop(8, 16)
     def _(i):
-        down_load(i).start()
+        down_load(i).start(priority=1)
 
     def gate_step(s):
         for copy in gate_load(s):

time: 45.9 us -> 45.9 us (level)
  no operation moved by 1% of the time
where the time goes in v2:
time: 45.9 us; the launch traced here: 45.7 us
  Pallas kernels  44.3 us (97%)
  local copies, waits for them, and re-layouts  1.38 us (3%)
    pallas_call x1, Pallas kernels, fused_device(): pl.pallas_call(fused_kernel, out_shape=jax.ShapeDtypeStruct((HALF, 1024),...  44.3 us
    unnamed x1, local copies, waits for them, and re-layouts  1.38 us

profile of v2, /device:TPU:0, one launch (start us, length us, event | category | flops | bytes accessed | tf_op | source)
XLA Modules:
  0.0 45.7 jit_solution(1407400664355634280)
XLA Ops:
  0.0 44.3 %decode_step.1 = bf16[16,1024]{1,0:T(8,128)(2,1)} custom-call(bf16[2,8192]{1,0:T(2,128)(2,1)} %queries.1, bf16[2,320,1024]{2,1,0:T(8,128)(2,1)} %keys.1, bf16[2,320,1024]{2,1,0:T(8,128)(2,1)} %values.1, s32[2]{0:T(128)} %lengths.1, s32[32]{0:T(128)} %slot_order.1, s32[16]{0:T(128)} %kept_rows.1, bf16[32,1024]{1,0:T(8,128)(2,1)} %residual.1, ...), custom_call_target="tpu_custom_call" | custom-call | flops 1946157056 | bytes 62914560 | tf_op jit(solution)/shard_map/decode_step/pallas_call | solution.py:391
  44.3 1.4 %copy.14 = bf16[16,1024]{1,0:T(8,128)(2,1)} copy(bf16[16,1024]{1,0:T(8,128)(2,1)} %decode_step.1) | data formatting | bytes 65536

commit v3 on v2

--- a/solution.py
+++ b/solution.py
@@ -101,7 +101,7 @@
     attn = lax.axis_index("attn")
     c = lax.axis_index("ffn")
     z, y = attn // 2, attn % 2
-    oz = lambda j: (z + j) % ZN
+    oz = lambda j: (z // 2 + j // 2) % 2 * 2 + (z % 2 + j % 2) % 2
     block = lambda zz, yy, cc: (zz * 2 + yy) * 2 + cc
     core_id = {"attn": attn, "ffn": 1 - c}
     y_id = {"attn": z * 2 + 1 - y, "ffn": c}

time: 45.9 us -> 47 us (1.024)
  Pallas kernels: 44.3 us -> 45.4 us
    pallas_call x1, Pallas kernels: 44.3 us -> 45.4 us  [fused_device(): pl.pallas_call(fused_kernel, out_shape=jax.ShapeDtypeStruct((HALF, 1024),...]
where the time goes in v3:
time: 47 us; the launch traced here: 46.8 us
  Pallas kernels  45.4 us (97%)
  local copies, waits for them, and re-layouts  1.38 us (3%)
    pallas_call x1, Pallas kernels, fused_device(): pl.pallas_call(fused_kernel, out_shape=jax.ShapeDtypeStruct((HALF, 1024),...  45.4 us
    unnamed x1, local copies, waits for them, and re-layouts  1.38 us

profile of v3, /device:TPU:0, one launch (start us, length us, event | category | flops | bytes accessed | tf_op | source)
XLA Modules:
  0.0 46.8 jit_solution(2484382327585890713)
XLA Ops:
  0.0 45.4 %decode_step.1 = bf16[16,1024]{1,0:T(8,128)(2,1)} custom-call(bf16[2,8192]{1,0:T(2,128)(2,1)} %queries.1, bf16[2,320,1024]{2,1,0:T(8,128)(2,1)} %keys.1, bf16[2,320,1024]{2,1,0:T(8,128)(2,1)} %values.1, s32[2]{0:T(128)} %lengths.1, s32[32]{0:T(128)} %slot_order.1, s32[16]{0:T(128)} %kept_rows.1, bf16[32,1024]{1,0:T(8,128)(2,1)} %residual.1, ...), custom_call_target="tpu_custom_call" | custom-call | flops 1946157056 | bytes 62914560 | tf_op jit(solution)/shard_map/decode_step/pallas_call | solution.py:391
  45.4 1.4 %copy.14 = bf16[16,1024]{1,0:T(8,128)(2,1)} copy(bf16[16,1024]{1,0:T(8,128)(2,1)} %decode_step.1) | data formatting | bytes 65536
